TPU v7x, 32 devices: a whole 2x2x4 slice. The times are simulated.
32 devices in a mesh: expert: 8 (over z, y), batch: 4 (over x, core).
Axes of the slice: x: 2, y: 2, z: 4, core: 2. Of those that a mesh axis runs over, the one named last changes fastest.
Arguments:
- tokens: bfloat16 [8192, 1024], P(('expert', 'batch')), may hold values from -6 to 6
- lengths: int32 [32], P(('expert', 'batch')), may hold values from 64 to 256, as said below
- expert_ids: int32 [8192], P(('expert', 'batch')), may hold values from 0 to 7, as said below
- slots: int32 [8192], P(('expert', 'batch')), may hold values from -1 to 31, as said below
- centroids: bfloat16 [8, 1024], replicated, may hold values from -0.125 to 0.125
- sublayer_norm_gain: bfloat16 [2, 8, 1024], P(None, 'expert'), may hold values from 0.5 to 1.5
- sublayer_norm_bias: bfloat16 [2, 8, 1024], P(None, 'expert'), may hold values from -0.59765625 to 0.59765625
- up_weight: bfloat16 [2, 8, 1024, 4096], P(None, 'expert', None, 'batch'), may hold values from -0.1875 to 0.1875
- up_bias: bfloat16 [2, 8, 4096], P(None, 'expert', 'batch'), may hold values from -0.59765625 to 0.59765625
- down_weight: bfloat16 [2, 8, 4096, 1024], P(None, 'expert', 'batch'), may hold values from -0.09375 to 0.09375
- down_bias: bfloat16 [2, 8, 1024], P(None, 'expert'), may hold values from -0.59765625 to 0.59765625
- cotangent: bfloat16 [8192, 1024], P(('expert', 'batch')), may hold values from -6 to 6
Outputs:
- mixed: bfloat16 [8192, 1024], P(('expert', 'batch'))
- tokens_grad: bfloat16 [8192, 1024], P(('expert', 'batch'))
- centroid_grad: float32 [8, 1024], replicated
- gain_grad: float32 [2, 8, 1024], P(None, 'expert')
- shift_grad: float32 [2, 8, 1024], P(None, 'expert')
- up_weight_grad: float32 [2, 8, 1024, 4096], P(None, 'expert', None, 'batch')
- up_bias_grad: float32 [2, 8, 4096], P(None, 'expert', 'batch')
- down_weight_grad: float32 [2, 8, 4096, 1024], P(None, 'expert', 'batch')
- down_bias_grad: float32 [2, 8, 1024], P(None, 'expert')
- gate_mass: float32 [8], replicated
- load: float32 [8], replicated
Inputs may be any that keep to these rules, and one draw needn't show every extreme that they name: `lengths`: one device's sequence has length 256 and one has 64. `expert_ids`: every expert is named somewhere. -1 exactly at padded positions; a device's live positions of one expert have distinct slots; some expert receives 32 positions from every device.
All inputs are finite; a program needn't handle non-finite values.
Results may differ from a plain program's by a relative error of at most 0.017.
Values may be sent and summed in bfloat16 or wider, within the bound.
A program may use at most 128 MiB of HBM per device.

v0:
```python
import functools

import jax
import jax.numpy as jnp
from jax import lax
from jax.experimental import pallas as pl
from jax.experimental.pallas import tpu as pltpu
from jax.sharding import PartitionSpec as P


def gelu_exact(values):
    return jax.nn.gelu(values, approximate=False)


def apply_layer_norm(row_block):
    values = row_block.astype(jnp.float32)
    row_mean = jnp.mean(values, axis=-1, keepdims=True)
    centered = values - row_mean
    row_inverse_scale = lax.rsqrt(jnp.mean(centered * centered, axis=-1, keepdims=True) + 1e-05)
    return (centered * row_inverse_scale, row_inverse_scale)


def per_device(
    tokens,
    lengths,
    expert_ids,
    slots,
    centroids,
    sublayer_norm_gain,
    sublayer_norm_bias,
    up_weight,
    up_bias,
    down_weight,
    down_bias,
    cotangent,
):
    tok_rows, width = tokens.shape
    layers = sublayer_norm_gain.shape[0]
    local_count = up_weight.shape[1]
    expert_count = centroids.shape[0]
    capacity = tok_rows // expert_count
    groups = lax.axis_size("expert")
    batches = lax.axis_size("batch")
    position = jnp.arange(tok_rows, dtype=jnp.int32)
    live = (position < lengths[0]).astype(jnp.float32)[:, None]
    target = jnp.where(slots >= 0, expert_ids * capacity + slots, tok_rows)
    source = jnp.full((tok_rows + 1,), -1, jnp.int32).at[target].set(position)[:tok_rows]
    filled = (source >= 0)[:, None]
    safe_source = jnp.maximum(source, 0)
    safe_target = jnp.minimum(target, tok_rows - 1)

    def pack(values):
        return jnp.where(filled, values[safe_source], jnp.zeros((), values.dtype))

    onehot = (expert_ids[:, None] == jnp.arange(expert_count, dtype=jnp.int32)[None, :]).astype(
        jnp.float32
    )
    logits = jnp.einsum("td,ed->te", tokens, centroids, preferred_element_type=jnp.float32)
    gate = jax.nn.sigmoid(jnp.sum(logits * onehot, axis=1))[:, None]
    used = onehot * live
    usage_gate = jnp.sum(used * gate, axis=0)
    usage_count = jnp.sum(used, axis=0)
    gate_total, count_total = lax.psum((usage_gate, usage_count), ("expert", "batch"))

    def expand_hidden(values, expert_layer_step):
        return values[expert_layer_step].astype(jnp.float32)[None, :, None, :]

    arrived = lax.all_to_all(pack(tokens), "expert", split_axis=0, concat_axis=0, tiled=True)
    current = arrived
    inputs = []
    kept = []
    for expert_layer_step in range(layers):
        gathered = lax.all_gather(current, "batch", axis=0, tiled=True)
        row_layout_grid = gathered.reshape(-1, local_count, capacity, width)
        standardized_input, row_inverse_scale = apply_layer_norm(row_layout_grid)
        normalized_rows = (
            standardized_input * expand_hidden(sublayer_norm_gain, expert_layer_step)
            + expand_hidden(sublayer_norm_bias, expert_layer_step)
        ).astype(jnp.bfloat16)
        pre_rows = jnp.einsum(
            "nlcd,ldf->nlcf",
            normalized_rows,
            up_weight[expert_layer_step],
            preferred_element_type=jnp.float32,
        ) + expand_hidden(up_bias, expert_layer_step)
        hidden_parts = (normalized_rows, pre_rows, gelu_exact(pre_rows).astype(jnp.bfloat16))

        def down_part(start, count, activity=hidden_parts[2], expert_layer_step=expert_layer_step):
            return jnp.einsum(
                "nlcf,lfd->nlcd",
                activity,
                down_weight[expert_layer_step],
                preferred_element_type=jnp.float32,
            )

        mixed_part = lax.psum_scatter(
            down_part(jnp.int32(0), lax.axis_size("batch") * groups).astype(jnp.bfloat16),
            "batch",
            scatter_dimension=0,
            tiled=True,
        ).astype(jnp.float32)
        own_grid = current.reshape(groups, local_count, capacity, width).astype(jnp.float32)
        result = (own_grid + mixed_part + expand_hidden(down_bias, expert_layer_step)).astype(
            jnp.bfloat16
        )
        inputs.append(current)
        kept.append(hidden_parts)
        current = result.reshape(tok_rows, width)
    returned = lax.all_to_all(current, "expert", split_axis=0, concat_axis=0, tiled=True)
    expert_tok = returned[safe_target].astype(jnp.float32)
    mixed = (live * (tokens.astype(jnp.float32) + gate * expert_tok)).astype(jnp.bfloat16)
    upstream = cotangent.astype(jnp.float32) * live
    gate_grad = jnp.sum(upstream * expert_tok, axis=1, keepdims=True)
    logit_grad = (gate_grad * gate * (1.0 - gate)).astype(jnp.bfloat16)
    route_grad = (onehot * logit_grad.astype(jnp.float32)).astype(jnp.bfloat16)
    centroid_part = jnp.einsum("te,td->ed", route_grad, tokens, preferred_element_type=jnp.float32)
    gate_input = jnp.einsum("te,ed->td", route_grad, centroids, preferred_element_type=jnp.float32)
    expert_grad = (gate * upstream).astype(jnp.bfloat16)
    grad_rows = lax.all_to_all(pack(expert_grad), "expert", split_axis=0, concat_axis=0, tiled=True)
    gain_parts = [None] * layers
    shift_parts = [None] * layers
    down_bias_parts = [None] * layers
    up_weight_grads = [None] * layers
    up_bias_grads = [None] * layers
    down_weight_grads = [None] * layers
    for expert_layer_step in range(layers - 1, -1, -1):
        own_rows = inputs[expert_layer_step]
        grads_all = lax.all_gather(grad_rows, "batch", axis=0, tiled=True).reshape(
            -1, local_count, capacity, width
        )
        normed, pre_act, activity = kept[expert_layer_step]
        act_grad = jnp.einsum(
            "nlcd,lfd->nlcf",
            grads_all,
            down_weight[expert_layer_step],
            preferred_element_type=jnp.float32,
        )
        pre_grad = jax.vjp(gelu_exact, pre_act)[1](act_grad)[0].astype(jnp.bfloat16)
        down_weight_grads[expert_layer_step] = jnp.einsum(
            "nlcf,nlcd->lfd", activity, grads_all, preferred_element_type=jnp.float32
        )
        up_weight_grads[expert_layer_step] = jnp.einsum(
            "nlcd,nlcf->ldf", normed, pre_grad, preferred_element_type=jnp.float32
        )
        up_bias_grads[expert_layer_step] = jnp.sum(pre_grad.astype(jnp.float32), axis=(0, 2))

        def up_part(start, count, pre_grad=pre_grad, expert_layer_step=expert_layer_step):
            return jnp.einsum(
                "nlcf,ldf->nlcd",
                pre_grad,
                up_weight[expert_layer_step],
                preferred_element_type=jnp.float32,
            )

        normed_grad = lax.psum_scatter(
            up_part(jnp.int32(0), lax.axis_size("batch") * groups).astype(jnp.bfloat16),
            "batch",
            scatter_dimension=0,
            tiled=True,
        ).astype(jnp.float32)
        out_grad = grad_rows.reshape(groups, local_count, capacity, width).astype(jnp.float32)
        down_bias_parts[expert_layer_step] = jnp.sum(out_grad, axis=(0, 2))
        own_hat, own_scale = apply_layer_norm(
            own_rows.reshape(groups, local_count, capacity, width)
        )
        gain_parts[expert_layer_step] = jnp.sum(normed_grad * own_hat, axis=(0, 2))
        shift_parts[expert_layer_step] = jnp.sum(normed_grad, axis=(0, 2))
        hat_grad = normed_grad * expand_hidden(sublayer_norm_gain, expert_layer_step)
        row_grad = own_scale * (
            hat_grad
            - jnp.mean(hat_grad, axis=-1, keepdims=True)
            - own_hat * jnp.mean(hat_grad * own_hat, axis=-1, keepdims=True)
        )
        grad_rows = (out_grad + row_grad).astype(jnp.bfloat16).reshape(tok_rows, width)
    gain_grad, shift_grad, down_bias_grad = lax.psum(
        (jnp.stack(gain_parts), jnp.stack(shift_parts), jnp.stack(down_bias_parts)), "batch"
    )
    token_back = lax.all_to_all(grad_rows, "expert", split_axis=0, concat_axis=0, tiled=True)
    tokens_grad = (
        upstream + gate_input + live * token_back[safe_target].astype(jnp.float32)
    ).astype(jnp.bfloat16)
    centroid_grad = lax.psum(centroid_part, ("expert", "batch"))
    denominator = jnp.float32(capacity * groups * batches)
    gate_mass = gate_total / denominator
    load = count_total / denominator
    return (
        mixed,
        tokens_grad,
        centroid_grad,
        gain_grad,
        shift_grad,
        jnp.stack(up_weight_grads),
        jnp.stack(up_bias_grads),
        jnp.stack(down_weight_grads),
        down_bias_grad,
        gate_mass,
        load,
    )


MESH = pl.DeviceIdType.MESH
F32 = jnp.float32
BF16 = jnp.bfloat16
ROW_STEP = 64
COL_STEP = 256
EMPTY = 8.0
LINK_KINDS = ("x", "g", "sum0", "out", "ngrad1", "ngrad0")
CORE_KINDS = ("x", "g", "part0", "h", "part1", "ngrad1", "hgrad", "ngrad0")
SCHEDULE = (
    "SX.0 SG.0 SX.1 SX.2",
    "SX.3 SX.4 PX.3 SX.5",
    "U0.3 SG.2 PX.0 D0.3",
    "SG.3 U0.0 SX.6 D0.0",
    "SX.7 PX.1 S0.0 SG.1",
    "U0.1 S0.3 D0.1 PX.2",
    "U0.2 SG.5 S0.1 PG.3",
    "H.3 PG.0 H.0 SG.4",
    "D0.2 SG.6 U1.3 D1.3",
    "U1.0 S0.2 H.1 PG.1",
    "SG.7 U1.1 B1.1 S1.1",
    "B1.3 PG.2 H.2 D1.1",
    "B1.0 SO.1 S1.0 U1.2",
    "B1.2 MX.1 HG.1 W1.1",
    "S1.2 D1.0 S1.3 D1.2",
    "HG.0 SO.2 B0.0 W1.3",
    "B0.1 SO.0 W1.2 HG.2",
    "B0.2 HG.3 MX.2 SQ.2",
    "SO.3 B0.3 SQ.1 SQ.0",
    "W0.0 TG.2 MX.0 MX.3",
    "R1.0 SQ.3 TG.1 W1.0",
    "R1.1 TG.0 TG.3 R1.2",
    "R0.0 W0.2 R0.1 W0.1",
    "W0.3 UP.1 R0.2 UP.0",
)
PART_SLOT = {"part0": 0, "part1": 0, "ngrad1": 1, "ngrad0": 1}
ROUTE_KINDS = ("x", "ct", "mixed", "tgrad", "totals")


def fused_fits(mesh):
    groups, batches = mesh.shape["expert"], mesh.shape["batch"]
    return batches == 4 and groups == 8


def rows_at(start, count, unit):
    return pl.ds(pl.multiple_of(start, unit), count)


def loop_rows(count, step, body):
    step = min(step, count)
    for start in range(0, count, step):
        body(start, step)


def loop_tiles(count, step, body):
    def one(i, carry):
        body(pl.multiple_of(i * step, step), step)
        return carry

    lax.fori_loop(0, count // step, one, 0)


def normalize(values):
    centered = values - jnp.mean(values, axis=-1, keepdims=True)
    scale = lax.rsqrt(jnp.mean(centered * centered, axis=-1, keepdims=True) + 1e-05)
    return centered * scale, scale


def dot(a, b, dims):
    return lax.dot_general(a, b, (dims, ((), ())), preferred_element_type=F32)


NN = ((1,), (0,))
NT = ((1,), (1,))
TN = ((0,), (0,))


def fused_kernel(
    groups,
    capacity,
    chunks,
    ids_ref,
    slots_ref,
    tok_ref,
    ct_ref,
    cent_ref,
    gain_ref,
    bias_ref,
    up_bias_ref,
    down_bias_ref,
    up_hbm,
    down_hbm,
    mixed_ref,
    tgrad_ref,
    totals_ref,
    small_ref,
    ub_ref,
    up_grad_ref,
    down_grad_ref,
    up_w,
    down_w,
    perm,
    pack_x,
    pack_ct,
    xa,
    ga,
    ha,
    hga,
    n_s,
    a_s,
    d_s,
    part,
    part_in,
    half_out,
    half_in,
    own_out,
    own_in,
    ct_own,
    gate_s,
    lg_s,
    back_out,
    back_in,
    acc,
    acc_0,
    red,
    totals_in,
    w_sem,
    route_send,
    route_recv,
    link_send,
    link_recv,
    core_send,
    core_recv,
    red_send,
    red_recv,
):
    tok_rows, width = tok_ref.shape
    hidden = up_w.shape[2]
    per = groups // chunks
    rows_m = per * 4 * capacity
    rows_h = rows_m // 2
    rows_o = rows_m // 4
    e = lax.axis_index("expert")
    b = lax.axis_index("batch")
    x = b // 2
    c = lax.rem(b, 2)
    sib = (e, x * 2 + (1 - c))
    far = (e, (1 - x) * 2 + c)

    def flipped(m):
        out = jnp.int32(0)
        bit = 1
        while bit < groups:
            digit = lax.rem(e // bit, 2)
            out = out + bit * ((1 - digit) if m & bit else digit)
            bit *= 2
        return out

    half = c * rows_h
    sib_half = (1 - c) * rows_h
    own = half + x * rows_o
    pairs = [tuple(range(j * per, (j + 1) * per)) for j in range(chunks)]
    order = pairs[1:] + pairs[:1]
    place = {m: (k, i) for k, ms in enumerate(order) for i, m in enumerate(ms)}
    others = range(1, groups)

    def at_half(k):
        return rows_at(k * rows_m + half, rows_h, rows_h)

    def at_sib_half(k):
        return rows_at(k * rows_m + sib_half, rows_h, rows_h)

    def at_block(m):
        k, i = place[m]
        return rows_at(k * rows_m + own + i * capacity, capacity, capacity)

    def at_all(k):
        return pl.ds(k * rows_m, rows_m)

    def copy_to(device, src, dst, send, recv):
        return pltpu.make_async_remote_copy(
            src_ref=src,
            dst_ref=dst,
            send_sem=send,
            recv_sem=recv,
            device_id=device,
            device_id_type=MESH,
        )

    def route(kind, m):
        n = ROUTE_KINDS.index(kind)
        k, i = place[m]
        to = flipped(m)
        theirs = rows_at(to * capacity, capacity, capacity)
        mine = rows_at(e * capacity, capacity, capacity)
        if kind == "x":
            src = pack_x.at[theirs]
            dst = xa.at[at_block(m)]
        elif kind == "ct":
            src = pack_ct.at[theirs]
            dst = ct_own.at[pl.ds(k * rows_o + i * capacity, capacity)]
        elif kind == "totals":
            src = dst = totals_in.at[e]
        else:
            s = 0 if kind == "mixed" else 1
            src = back_out.at[s, pl.ds(k * rows_o + i * capacity, capacity)]
            dst = back_in.at[s, mine]
        return copy_to((to, b), src, dst, route_send.at[n, m], route_recv.at[n, m])

    def link(kind, k):
        n = LINK_KINDS.index(kind)
        if kind in ("x", "g"):
            src = dst = {"x": xa, "g": ga}[kind].at[at_block(k)]
        elif kind in ("sum0", "ngrad1"):
            s = 0 if kind == "sum0" else 1
            at = pl.ds(k * rows_h, rows_h)
            src, dst = half_out.at[s, at], half_in.at[s, at]
        else:
            s = 0 if kind == "out" else 1
            at = pl.ds(k * rows_o, rows_o)
            src, dst = own_out.at[s, at], own_in.at[s, at]
        return copy_to(far, src, dst, link_send.at[n, k], link_recv.at[n, k])

    def core(kind, k):
        n = CORE_KINDS.index(kind)
        whole = {"x": xa, "g": ga, "h": ha, "hgrad": hga}
        if kind in whole:
            src = dst = whole[kind].at[at_half(k)]
        else:
            s = PART_SLOT[kind]
            src = part.at[s, at_sib_half(k)]
            dst = part_in.at[s, pl.ds(k * rows_h, rows_h)]
        return copy_to(sib, src, dst, core_send.at[n, k], core_recv.at[n, k])

    barrier = pltpu.get_barrier_semaphore()
    peers = [sib, far] + [(flipped(m), b) for m in range(1, groups)]
    for peer in peers:
        pl.semaphore_signal(barrier, inc=1, device_id=peer, device_id_type=MESH)
    loads = []
    for j in range(2):
        loads.append(pltpu.make_async_copy(up_hbm.at[j, 0], up_w.at[j], w_sem.at[2 * j]))
        loads.append(pltpu.make_async_copy(down_hbm.at[j, 0], down_w.at[j], w_sem.at[2 * j + 1]))
    for load in loads:
        load.start()
    target = jnp.where(
        slots_ref[...] >= 0, ids_ref[...] * capacity + slots_ref[...], -1
    )
    slot = lax.broadcasted_iota(jnp.int32, (tok_rows, tok_rows), 0)
    onehot = jnp.where(slot == target, 1.0, 0.0)
    perm[...] = onehot.astype(BF16)
    empty = EMPTY * (1.0 - jnp.sum(onehot, axis=1, keepdims=True))

    def pack(start, step):
        cols = rows_at(start, step, step)
        pack_x[:, cols] = (dot(perm[...], tok_ref[:, cols], NN) + empty).astype(BF16)
        pack_ct[:, cols] = dot(perm[...], ct_ref[:, cols], NN).astype(BF16)

    loop_rows(width, COL_STEP, pack)
    acc[...] = jnp.zeros_like(acc)
    acc_0[...] = jnp.zeros_like(acc_0)
    cent_rows = cent_ref[...].astype(F32)
    cent_at = lax.broadcasted_iota(jnp.int32, cent_rows.shape, 0)
    cent = jnp.sum(jnp.where(cent_at == e, cent_rows, 0.0), axis=0, keepdims=True)
    pl.semaphore_wait(barrier, len(peers))
    near = 2 * per
    for kind, masks in (
        ("x", range(1, near)),
        ("ct", range(1, per)),
        ("x", range(near, groups)),
        ("ct", range(per, groups)),
    ):
        for m in masks:
            route(kind, m).start()
    mine = rows_at(e * capacity, capacity, capacity)
    xa[at_block(0)] = pack_x[mine]
    first_k, first_i = place[0]
    ct_own[pl.ds(first_k * rows_o + first_i * capacity, capacity)] = pack_ct[mine]

    def send_x(m):
        if m:
            route("x", m).wait_recv()
        link("x", m).start()

    def send_g(m):
        if m:
            route("ct", m).wait_recv()
        k, i = place[m]
        at_o = pl.ds(k * rows_o + i * capacity, capacity)
        values = xa[at_block(m)].astype(F32)
        gate = jax.nn.sigmoid(jnp.sum(values * cent, axis=-1, keepdims=True))
        gate_s[at_o] = jnp.broadcast_to(gate, (capacity, 128))
        ga[at_block(m)] = (gate * ct_own[at_o].astype(F32)).astype(BF16)
        used = jnp.where(values[:, 0:1] < 7.0, 1.0, 0.0)
        acc[3:4] += jnp.broadcast_to(jnp.sum(used * gate, axis=0, keepdims=True), (1, width))
        acc[4:5] += jnp.broadcast_to(jnp.sum(used, axis=0, keepdims=True), (1, width))
        link("g", m).start()

    def spread(kind, k):
        for m in order[k]:
            link(kind, m).wait_recv()
        core(kind, k).start()

    def up_step(j, rows_ref, k):
        gain = gain_ref[j : j + 1].astype(F32)
        bias = bias_ref[j : j + 1].astype(F32)

        def norm(start, step):
            at = rows_at(k * rows_m + start, step, step)
            rhat, _ = normalize(rows_ref[at].astype(F32))
            n_s[j, at] = (rhat * gain + bias).astype(BF16)

        loop_tiles(rows_m, 2 * ROW_STEP, norm)

        def up(start, step):
            cols = rows_at(start, step, step)
            pre = dot(n_s[j, at_all(k)], up_w[j, :, cols], NN) + up_bias_ref[j : j + 1, cols].astype(
                F32
            )
            cdf = 0.5 * (1.0 + lax.erf(pre * (0.5**0.5)))
            pdf = jnp.exp(-0.5 * pre * pre) * 0.3989422804014327
            a_s[j, at_all(k), cols] = (pre * cdf).astype(BF16)
            d_s[j, at_all(k), cols] = (cdf + pre * pdf).astype(BF16)

        loop_tiles(hidden, 2 * COL_STEP, up)

    def down_step(j, k):
        kind = "part%d" % j
        if j == 1:
            core("part0", k).wait_send()

        def down(start, step):
            cols = rows_at(start, step, step)
            part[0, at_all(k), cols] = dot(a_s[j, at_all(k)], down_w[j, :, cols], NN).astype(BF16)

        loop_tiles(width, 2 * COL_STEP, down)
        core(kind, k).start()

    def back_step(j, grads_ref, k):
        kind = "ngrad%d" % j
        if j == 0:
            core("ngrad1", k).wait_send()

        def act(start, step):
            cols = rows_at(start, step, step)
            grad = dot(grads_ref[at_all(k)], down_w[j, cols, :], NT)
            d_s[j, at_all(k), cols] = (grad * d_s[j, at_all(k), cols].astype(F32)).astype(BF16)

        loop_tiles(hidden, 2 * COL_STEP, act)

        def up_back(start, step):
            cols = rows_at(start, step, step)
            part[1, at_all(k), cols] = dot(d_s[j, at_all(k)], up_w[j, cols, :], NT).astype(BF16)

        loop_tiles(width, 2 * COL_STEP, up_back)
        core(kind, k).start()

    def sum_half(kind, link_kind, k):
        s = PART_SLOT[kind]
        o = ("sum0", "ngrad1").index(link_kind)
        core(kind, k).wait_recv()

        def add_half(start, step):
            at = rows_at(k * rows_m + half + start, step, step)
            at_h = rows_at(k * rows_h + start, step, step)
            total = part[s, at].astype(F32) + part_in[s, at_h].astype(F32)
            half_out[o, at_h] = total.astype(BF16)

        loop_rows(rows_h, ROW_STEP, add_half)
        link(link_kind, k).start()

    def sum_far(kind, link_kind, k):
        s = PART_SLOT[kind]
        o = ("out", "ngrad0").index(link_kind)
        core(kind, k).wait_recv()

        def add_far(start, step):
            at = rows_at(k * rows_m + half + (1 - x) * rows_o + start, step, step)
            at_h = rows_at(k * rows_h + (1 - x) * rows_o + start, step, step)
            at_o = rows_at(k * rows_o + start, step, step)
            total = part[s, at].astype(F32) + part_in[s, at_h].astype(F32)
            own_out[o, at_o] = total.astype(BF16)

        loop_rows(rows_o, ROW_STEP, add_far)
        link(link_kind, k).start()

    def sum_own(s, o, k, start, step):
        at = rows_at(k * rows_m + own + start, step, step)
        at_h = rows_at(k * rows_h + x * rows_o + start, step, step)
        at_o = rows_at(k * rows_o + start, step, step)
        mine = part[s, at].astype(F32) + part_in[s, at_h].astype(F32)
        return mine + own_in[o, at_o].astype(F32)

    def make_h(k):
        link("sum0", k).wait_recv()
        shift = down_bias_ref[0:1].astype(F32)

        def add_h(start, step):
            at = rows_at(k * rows_m + half + start, step, step)
            at_h = rows_at(k * rows_h + start, step, step)
            total = half_out[0, at_h].astype(F32) + half_in[0, at_h].astype(F32)
            ha[at] = (xa[at].astype(F32) + total + shift).astype(BF16)

        loop_rows(rows_h, ROW_STEP, add_h)
        core("h", k).start()

    def norm_back(rows, ngrad, gain):
        rhat, scale = normalize(rows)
        q = ngrad * gain
        back = scale * (
            q - jnp.mean(q, axis=-1, keepdims=True) - rhat * jnp.mean(q * rhat, axis=-1, keepdims=True)
        )
        return back, rhat

    def make_hgrad(k):
        link("ngrad1", k).wait_recv()
        gain = gain_ref[1:2].astype(F32)

        def grad_h(start, step):
            at = rows_at(k * rows_m + half + start, step, step)
            at_h = rows_at(k * rows_h + start, step, step)
            ngrad = half_out[1, at_h].astype(F32) + half_in[1, at_h].astype(F32)
            back, rhat = norm_back(ha[at].astype(F32), ngrad, gain)
            hga[at] = (ga[at].astype(F32) + back).astype(BF16)
            acc[0:1] += 0.5 * jnp.sum(ngrad * rhat, axis=0, keepdims=True)
            acc[1:2] += 0.5 * jnp.sum(ngrad, axis=0, keepdims=True)

        loop_tiles(rows_h, ROW_STEP, grad_h)
        core("hgrad", k).start()

    def give_back(kind, k):
        for m in order[k]:
            if m:
                route(kind, m).start()
            else:
                s = 0 if kind == "mixed" else 1
                _, i = place[0]
                back_in[s, mine] = back_out[s, pl.ds(k * rows_o + i * capacity, capacity)]

    def make_mixed(k):
        link("out", k).wait_recv()
        shift = down_bias_ref[1:2].astype(F32)

        def mix(start, step):
            at = rows_at(k * rows_m + own + start, step, step)
            at_o = rows_at(k * rows_o + start, step, step)
            out = (ha[at].astype(F32) + sum_own(0, 0, k, start, step) + shift).astype(BF16).astype(F32)
            rows = xa[at].astype(F32)
            gate = gate_s[at_o][:, 0:1]
            back_out[0, at_o] = (rows + gate * out).astype(BF16)
            along = jnp.sum(ct_own[at_o].astype(F32) * out, axis=-1, keepdims=True)
            lgrad = (along * gate * (1.0 - gate)).astype(BF16).astype(F32)
            lg_s[at_o] = jnp.broadcast_to(lgrad, (step, 128))
            acc[2:3] += jnp.sum(lgrad * rows, axis=0, keepdims=True)

        loop_rows(rows_o, ROW_STEP, mix)
        give_back("mixed", k)

    def make_tgrad(k):
        link("ngrad0", k).wait_recv()
        gain = gain_ref[0:1].astype(F32)

        def grad_t(start, step):
            at = rows_at(k * rows_m + own + start, step, step)
            at_o = rows_at(k * rows_o + start, step, step)
            ngrad = sum_own(1, 1, k, start, step)
            back, rhat = norm_back(xa[at].astype(F32), ngrad, gain)
            back = (hga[at].astype(F32) + back).astype(BF16).astype(F32)
            back_out[1, at_o] = (
                ct_own[at_o].astype(F32) + lg_s[at_o][:, 0:1] * cent + back
            ).astype(BF16)
            acc_0[0:1] += jnp.sum(ngrad * rhat, axis=0, keepdims=True)
            acc_0[1:2] += jnp.sum(ngrad, axis=0, keepdims=True)

        loop_rows(rows_o, ROW_STEP, grad_t)
        give_back("tgrad", k)

    def column_sums(rows_ref):
        def one(i, total):
            values = rows_ref[rows_at(i * ROW_STEP, ROW_STEP, ROW_STEP)].astype(F32)
            return total + jnp.sum(values, axis=0, keepdims=True)

        return lax.fori_loop(
            0, rows_ref.shape[0] // ROW_STEP, one, jnp.zeros((1, rows_ref.shape[1]), F32)
        )

    def weight_grad(j, q):
        grads_ref = (hga, ga)[j]
        into, left, right = (
            (down_grad_ref, a_s.at[j], grads_ref),
            (up_grad_ref, n_s.at[j], d_s.at[j]),
        )[q // 2]
        if q == 0:
            small_ref[4 + j : 5 + j] = column_sums(right)
        if q == 2:
            ub_ref[j : j + 1] = column_sums(right)
        count = left.shape[1] // 2

        def tile(start, step):
            at = rows_at(q % 2 * count + start, step, step)
            into[j, 0, at] = dot(left[:, at], right[...], TN).astype(BF16)

        loop_tiles(count, COL_STEP, tile)

    def over(s):
        return copy_to(sib, red.at[s, 0], red.at[s, 1], red_send.at[s, 0], red_recv.at[s, 0])

    def across(s):
        return copy_to(far, red.at[s, 0], red.at[s, 2], red_send.at[s, 1], red_recv.at[s, 1])

    def total(s, step):
        if step == 0:
            red[s, 0] = (acc, acc_0)[s][...]
            over(s).start()
        elif step == 1:
            over(s).wait()
            red[s, 0] = red[s, 0] + red[s, 1]
            across(s).start()
        else:
            across(s).wait()
            sums = red[s, 0] + red[s, 2]
            if s == 0:
                small_ref[1:2] = sums[0:1]
                small_ref[3:4] = sums[1:2]
                for i in range(width // 128):
                    totals_in[e, i : i + 1] = sums[2:3, i * 128 : (i + 1) * 128]
                totals_in[e, 8:10] = sums[3:5, 0:128]
                for m in others:
                    route("totals", m).start()
            else:
                small_ref[0:1] = sums[0:1]
                small_ref[2:3] = sums[1:2]

    def unpack(s):
        kind, out_ref = (("mixed", mixed_ref), ("tgrad", tgrad_ref))[s]
        for m in others:
            route(kind, m).wait_recv()

        def place_tokens(start, step):
            cols = rows_at(start, step, step)
            out_ref[:, cols] = dot(perm[...], back_in[s, :, cols], TN).astype(BF16)

        loop_rows(width, COL_STEP, place_tokens)

    steps = range(chunks)

    def up_0(k):
        if k == first_use[0]:
            loads[0].wait()
        core("x", k).wait_recv()
        up_step(0, xa, k)

    def down_0(k):
        if k == first_use[2]:
            loads[1].wait()
        down_step(0, k)

    def up_1(k):
        if k == first_use[1]:
            loads[2].wait()
            loads[3].wait()
        core("h", k).wait_recv()
        up_step(1, ha, k)

    def back_1(k):
        core("g", k).wait_recv()
        back_step(1, ga, k)

    def back_0(k):
        core("hgrad", k).wait_recv()
        back_step(0, hga, k)

    tasks = {
        "SX": send_x,
        "SG": send_g,
        "PX": functools.partial(spread, "x"),
        "PG": functools.partial(spread, "g"),
        "U0": up_0,
        "D0": down_0,
        "S0": functools.partial(sum_half, "part0", "sum0"),
        "H": make_h,
        "U1": up_1,
        "B1": back_1,
        "D1": functools.partial(down_step, 1),
        "S1": functools.partial(sum_half, "ngrad1", "ngrad1"),
        "SO": functools.partial(sum_far, "part1", "out"),
        "HG": make_hgrad,
        "MX": make_mixed,
        "B0": back_0,
        "SQ": functools.partial(sum_far, "ngrad0", "ngrad0"),
        "TG": make_tgrad,
        "W1": functools.partial(weight_grad, 1),
        "W0": functools.partial(weight_grad, 0),
        "R1": functools.partial(total, 0),
        "R0": functools.partial(total, 1),
        "UP": unpack,
    }
    plan = [word.split(".") for line in SCHEDULE for word in line.split()]
    first_use = [next(int(k) for name, k in plan if name == u) for u in ("U0", "U1", "D0")]
    for name, k in plan:
        tasks[name](int(k))

    for m in others:
        route("totals", m).wait_recv()
    totals_ref[...] = totals_in[...]
    for m in others:
        for kind in ROUTE_KINDS:
            route(kind, m).wait_send()
    for m in range(groups):
        for kind in LINK_KINDS[:2]:
            link(kind, m).wait_send()
    for k in steps:
        for kind in LINK_KINDS[2:]:
            link(kind, k).wait_send()
        for kind in CORE_KINDS:
            if kind not in ("part0", "ngrad1"):
                core(kind, k).wait_send()


def widen_kernel(
    denominator,
    mixed_ref,
    tgrad_ref,
    totals_ref,
    small_ref,
    ub_ref,
    up_ref,
    down_ref,
    mixed_out,
    tgrad_out,
    cent_out,
    gain_out,
    shift_out,
    up_out,
    ub_out,
    down_out,
    db_out,
    mass_out,
    load_out,
    up_wide,
    down_wide,
    row_sem,
    out_sem,
):
    layers, tiles, rows = up_wide.shape[:3]
    leaving = [
        pltpu.make_async_copy(mixed_ref, mixed_out, row_sem.at[0]),
        pltpu.make_async_copy(tgrad_ref, tgrad_out, row_sem.at[1]),
    ]
    for move in leaving:
        move.start()
    for j in range(layers):
        for n, (src, wide, dst) in enumerate(
            ((down_ref, down_wide, down_out), (up_ref, up_wide, up_out))
        ):
            for t in range(tiles):
                at = pl.ds(t * rows, rows)
                wide[j, t] = src[j, 0, at].astype(F32)
                move = pltpu.make_async_copy(wide.at[j, t], dst.at[j, 0, at], out_sem.at[n, j, t])
                move.start()
                leaving.append(move)
    for i in range(cent_out.shape[1] // 128):
        cent_out[:, i * 128 : (i + 1) * 128] = totals_ref[:, i]
    for j in range(layers):
        gain_out[j] = small_ref[j : j + 1]
        shift_out[j] = small_ref[2 + j : 3 + j]
        db_out[j] = small_ref[4 + j : 5 + j]
        ub_out[j] = ub_ref[j : j + 1]
    experts = totals_ref.shape[0]
    diagonal = lax.broadcasted_iota(jnp.int32, (experts, 128), 0) == lax.broadcasted_iota(
        jnp.int32, (experts, 128), 1
    )
    for out, n in ((mass_out, 8), (load_out, 9)):
        values = jnp.sum(jnp.where(diagonal, totals_ref[:, n], 0.0), axis=0)
        out[...] = values[0:experts] / jnp.float32(denominator)
    for move in leaving:
        move.wait()


def per_device_fused(
    tokens,
    lengths,
    expert_ids,
    slots,
    centroids,
    sublayer_norm_gain,
    sublayer_norm_bias,
    up_weight,
    up_bias,
    down_weight,
    down_bias,
    cotangent,
):
    tok_rows, width = tokens.shape
    groups = lax.axis_size("expert")
    batches = lax.axis_size("batch")
    experts = centroids.shape[0]
    capacity = tok_rows // experts
    hidden = up_weight.shape[3]
    chunks = 4
    total = groups * batches * capacity
    def flat(values):
        return values.reshape(values.shape[0], -1)

    vmem = pl.BlockSpec(memory_space=pltpu.VMEM)
    hbm = pl.BlockSpec(memory_space=pl.ANY)
    outs = pl.pallas_call(
        functools.partial(fused_kernel, groups, capacity, chunks),
        out_shape=[
            pltpu.VMEM((tok_rows, width), BF16),
            pltpu.VMEM((tok_rows, width), BF16),
            pltpu.VMEM((groups, 16, 128), F32),
            pltpu.VMEM((8, width), F32),
            pltpu.VMEM((8, hidden), F32),
            pltpu.VMEM(up_weight.shape, BF16),
            pltpu.VMEM(down_weight.shape, BF16),
        ],
        in_specs=[vmem] * 9 + [hbm] * 2,
        out_specs=[vmem] * 7,
        scratch_shapes=[
            pltpu.VMEM((2, width, hidden), BF16),
            pltpu.VMEM((2, hidden, width), BF16),
            pltpu.VMEM((tok_rows, tok_rows), BF16),
            pltpu.VMEM((tok_rows, width), BF16),
            pltpu.VMEM((tok_rows, width), BF16),
            pltpu.VMEM((total, width), BF16),
            pltpu.VMEM((total, width), BF16),
            pltpu.VMEM((total, width), BF16),
            pltpu.VMEM((total, width), BF16),
            pltpu.VMEM((2, total, width), BF16),
            pltpu.VMEM((2, total, hidden), BF16),
            pltpu.VMEM((2, total, hidden), BF16),
            pltpu.VMEM((2, total, width), BF16),
            pltpu.VMEM((2, total // 2, width), BF16),
            pltpu.VMEM((2, total // 2, width), BF16),
            pltpu.VMEM((2, total // 2, width), BF16),
            pltpu.VMEM((2, total // 4, width), BF16),
            pltpu.VMEM((2, total // 4, width), BF16),
            pltpu.VMEM((tok_rows, width), BF16),
            pltpu.VMEM((tok_rows, 128), F32),
            pltpu.VMEM((tok_rows, 128), F32),
            pltpu.VMEM((2, tok_rows, width), BF16),
            pltpu.VMEM((2, tok_rows, width), BF16),
            pltpu.VMEM((8, width), F32),
            pltpu.VMEM((8, width), F32),
            pltpu.VMEM((2, 3, 8, width), F32),
            pltpu.VMEM((groups, 16, 128), F32),
            pltpu.SemaphoreType.DMA((4,)),
            pltpu.SemaphoreType.DMA((len(ROUTE_KINDS), groups)),
            pltpu.SemaphoreType.DMA((len(ROUTE_KINDS), groups)),
            pltpu.SemaphoreType.DMA((len(LINK_KINDS), groups)),
            pltpu.SemaphoreType.DMA((len(LINK_KINDS), groups)),
            pltpu.SemaphoreType.DMA((len(CORE_KINDS), chunks)),
            pltpu.SemaphoreType.DMA((len(CORE_KINDS), chunks)),
            pltpu.SemaphoreType.DMA((2, 2)),
            pltpu.SemaphoreType.DMA((2, 2)),
        ],
        compiler_params=pltpu.CompilerParams(
            collective_id=0, has_side_effects=True, vmem_limit_bytes=52 << 20
        ),
        cost_estimate=pl.CostEstimate(
            flops=24 * total * width * hidden, bytes_accessed=40 << 20, transcendentals=0
        ),
    )(
        expert_ids.reshape(1, tok_rows),
        slots.reshape(1, tok_rows),
        tokens,
        cotangent,
        centroids,
        flat(sublayer_norm_gain),
        flat(sublayer_norm_bias),
        flat(up_bias),
        flat(down_bias),
        up_weight,
        down_weight,
    )
    layers = up_weight.shape[0]
    tiles = 4
    row = jax.ShapeDtypeStruct((layers, 1, width), F32)
    return pl.pallas_call(
        functools.partial(widen_kernel, capacity * groups * batches),
        out_shape=[
            jax.ShapeDtypeStruct(tokens.shape, BF16),
            jax.ShapeDtypeStruct(tokens.shape, BF16),
            jax.ShapeDtypeStruct((experts, width), F32),
            row,
            row,
            jax.ShapeDtypeStruct(up_weight.shape, F32),
            jax.ShapeDtypeStruct((layers, 1, hidden), F32),
            jax.ShapeDtypeStruct(down_weight.shape, F32),
            row,
            jax.ShapeDtypeStruct((experts,), F32),
            jax.ShapeDtypeStruct((experts,), F32),
        ],
        in_specs=[vmem] * 7,
        out_specs=[hbm, hbm, vmem, vmem, vmem, hbm, vmem, hbm, vmem, vmem, vmem],
        scratch_shapes=[
            pltpu.VMEM((layers, tiles, width // tiles, hidden), F32),
            pltpu.VMEM((layers, tiles, hidden // tiles, width), F32),
            pltpu.SemaphoreType.DMA((2,)),
            pltpu.SemaphoreType.DMA((2, layers, tiles)),
        ],
        compiler_params=pltpu.CompilerParams(vmem_limit_bytes=24 << 20),
        cost_estimate=pl.CostEstimate(
            flops=0, bytes_accessed=12 * layers * width * hidden, transcendentals=0
        ),
    )(*(pltpu.with_memory_space_constraint(out, pltpu.VMEM) for out in outs))


def solution(mesh):
    in_specs = (
        P(("expert", "batch"), None),
        P(("expert", "batch")),
        P(("expert", "batch")),
        P(("expert", "batch")),
        P(),
        P(None, "expert", None),
        P(None, "expert", None),
        P(None, "expert", None, "batch"),
        P(None, "expert", "batch"),
        P(None, "expert", "batch", None),
        P(None, "expert", None),
        P(("expert", "batch"), None),
    )
    out_specs = (
        P(("expert", "batch"), None),
        P(("expert", "batch"), None),
        P(),
        P(None, "expert", None),
        P(None, "expert", None),
        P(None, "expert", None, "batch"),
        P(None, "expert", "batch"),
        P(None, "expert", "batch", None),
        P(None, "expert", None),
        P(),
        P(),
    )
    body = per_device_fused if fused_fits(mesh) else per_device
    return jax.shard_map(
        body, mesh=mesh, in_specs=in_specs, out_specs=out_specs, check_vma=False
    )
```

profile of v0, /device:TPU:0, one launch (start us, length us, event | category | flops | bytes accessed | tf_op | source)
XLA Modules:
  0.0 120.0 jit_solution(5036638346739900164)
XLA Ops:
  0.6 112.2 %shard_map.194 = (bf16[256,1024]{1,0:T(8,128)(2,1)S(1)}, bf16[256,1024]{1,0:T(8,128)(2,1)S(1)}, f32[8,16,128]{2,1,0:T(8,128)S(1)}, f32[8,1024]{1,0:T(8,128)S(1)}...) custom-call(s32[1,256]{1,0:T(1,128)} %bitcast.10, ...), custom_call_target="tpu_custom_call" | custom-call | flops 25769803776 | bytes 41943040 | tf_op jit(solution)/shard_map/pallas_call | solution.py:905
  112.8 7.0 %shard_map.195 = (bf16[256,1024]{1,0:T(8,128)(2,1)}, bf16[256,1024]{1,0:T(8,128)(2,1)}, f32[8,1024]{1,0:T(8,128)}, f32[2,1,1024]{2,1,0:T(1,128)}, f32[2,1,1024]{...) custom-call(bf16[256,1024]{1,0:T(8,128)(2,1)S(1)} %get-tuple-element, ...), custom_call_target="tpu_custom_call" | custom-call | bytes 25165824 | tf_op jit(solution)/shard_map/pallas_call | solution.py:978
where the time goes:
time: 120 us
  Pallas kernels  119 us (99%)
    pallas_call x1, Pallas kernels, per_device_fused(): pl.pallas_call(functools.partial(fused_kernel, groups, capacity, chunks),...  112 us
    pallas_call x1, Pallas kernels, per_device_fused(): pl.pallas_call(functools.partial(widen_kernel, capacity * groups * batche...  7 us

commit v1 on v0

--- a/solution.py
+++ b/solution.py
@@ -204,41 +204,52 @@
 ROW_STEP = 64
 COL_STEP = 256
 EMPTY = 8.0
-LINK_KINDS = ("x", "g", "sum0", "out", "ngrad1", "ngrad0")
+BLOCK_KINDS = ("x", "g", "ngrad0")
+LINK_KINDS = BLOCK_KINDS + ("sum0", "out", "ngrad1")
 CORE_KINDS = ("x", "g", "part0", "h", "part1", "ngrad1", "hgrad", "ngrad0")
 SCHEDULE = (
     "SX.0 SG.0 SX.1 SX.2",
-    "SX.3 SX.4 PX.3 SX.5",
-    "U0.3 SG.2 PX.0 D0.3",
-    "SG.3 U0.0 SX.6 D0.0",
-    "SX.7 PX.1 S0.0 SG.1",
-    "U0.1 S0.3 D0.1 PX.2",
-    "U0.2 SG.5 S0.1 PG.3",
-    "H.3 PG.0 H.0 SG.4",
-    "D0.2 SG.6 U1.3 D1.3",
-    "U1.0 S0.2 H.1 PG.1",
-    "SG.7 U1.1 B1.1 S1.1",
-    "B1.3 PG.2 H.2 D1.1",
-    "B1.0 SO.1 S1.0 U1.2",
-    "B1.2 MX.1 HG.1 W1.1",
-    "S1.2 D1.0 S1.3 D1.2",
-    "HG.0 SO.2 B0.0 W1.3",
-    "B0.1 SO.0 W1.2 HG.2",
-    "B0.2 HG.3 MX.2 SQ.2",
-    "SO.3 B0.3 SQ.1 SQ.0",
-    "W0.0 TG.2 MX.0 MX.3",
-    "R1.0 SQ.3 TG.1 W1.0",
-    "R1.1 TG.0 TG.3 R1.2",
-    "R0.0 W0.2 R0.1 W0.1",
-    "W0.3 UP.1 R0.2 UP.0",
+    "SX.3 SX.4 SX.5 SG.2",
+    "SG.1 PX.0 U0.0 SX.6",
+    "SG.3 D0.0 PX.1 S0.0",
+    "U0.1 D0.1 PX.3 SX.7",
+    "SG.5 S0.1 PX.2 H.0",
+    "PG.3 U0.3 PG.0 SG.4",
+    "U0.2 D0.2 SG.7 D0.3",
+    "SG.6 PG.1 S0.2 U1.0",
+    "PG.2 H.1 S0.3 U1.1",
+    "B1.0 D1.1 H.2 S1.0",
+    "B1.1 U1.2 S1.1 H.3",
+    "SO.1 B1.2 U1.3 B1.3",
+    "W1.2 S1.2 D1.0 HG.1",
+    "HG.0 W1.0 SO.0 B0.1",
+    "B0.0 MX.1 SQ.1 GS.1",
+    "S1.3 HG.2 W1.3 B0.2",
+    "D1.2 D1.3 SO.2 TG.5",
+    "TG.4 MX.0 SQ.2 GS.2",
+    "HG.3 SO.3 SQ.0 GS.0",
+    "W1.1 MX.2 B0.3 TG.7",
+    "TG.6 SQ.3 GS.3 R0.0",
+    "MX.3 R1.0 R1.1 TG.3",
+    "TG.2 TG.1 TG.0 R1.2",
+    "UP.0 R0.1 R0.2 UP.1",
 )
 PART_SLOT = {"part0": 0, "part1": 0, "ngrad1": 1, "ngrad0": 1}
 ROUTE_KINDS = ("x", "ct", "mixed", "tgrad", "totals")
 
 
-def fused_fits(mesh):
-    groups, batches = mesh.shape["expert"], mesh.shape["batch"]
-    return batches == 4 and groups == 8
+def fused_fits(tokens, centroids, up_weight):
+    tok_rows, width = tokens.shape
+    groups, capacity = lax.axis_size("expert"), tok_rows // centroids.shape[0]
+    return (
+        lax.axis_size("batch") == 4
+        and groups == 8
+        and up_weight.shape[:2] == (2, 1)
+        and centroids.shape[0] == groups
+        and up_weight.shape[3] == width
+        and width % (4 * COL_STEP) == 0
+        and capacity % 32 == 0
+    )
 
 
 def rows_at(start, count, unit):
@@ -293,9 +304,12 @@
     tgrad_ref,
     totals_ref,
     small_ref,
-    ub_ref,
     up_grad_ref,
     down_grad_ref,
+    n_0,
+    a_0,
+    d_0,
+    hg_0,
     up_w,
     down_w,
     perm,
@@ -305,9 +319,9 @@
     ga,
     ha,
     hga,
-    n_s,
-    a_s,
-    d_s,
+    n_1,
+    a_1,
+    d_1,
     part,
     part_in,
     half_out,
@@ -335,6 +349,7 @@
 ):
     tok_rows, width = tok_ref.shape
     hidden = up_w.shape[2]
+    n_s, a_s, d_s = (n_0, n_1), (a_0, a_1), (d_0, d_1)
     per = groups // chunks
     rows_m = per * 4 * capacity
     rows_h = rows_m // 2
@@ -366,6 +381,10 @@
     def at_half(k):
         return rows_at(k * rows_m + half, rows_h, rows_h)
 
+    def at_own_block(m):
+        k, i = place[m]
+        return pl.ds(k * rows_o + i * capacity, capacity)
+
     def at_sib_half(k):
         return rows_at(k * rows_m + sib_half, rows_h, rows_h)
 
@@ -388,7 +407,6 @@
 
     def route(kind, m):
         n = ROUTE_KINDS.index(kind)
-        k, i = place[m]
         to = flipped(m)
         theirs = rows_at(to * capacity, capacity, capacity)
         mine = rows_at(e * capacity, capacity, capacity)
@@ -397,12 +415,12 @@
             dst = xa.at[at_block(m)]
         elif kind == "ct":
             src = pack_ct.at[theirs]
-            dst = ct_own.at[pl.ds(k * rows_o + i * capacity, capacity)]
+            dst = ct_own.at[at_own_block(m)]
         elif kind == "totals":
             src = dst = totals_in.at[e]
         else:
             s = 0 if kind == "mixed" else 1
-            src = back_out.at[s, pl.ds(k * rows_o + i * capacity, capacity)]
+            src = back_out.at[s, at_own_block(m)]
             dst = back_in.at[s, mine]
         return copy_to((to, b), src, dst, route_send.at[n, m], route_recv.at[n, m])
 
@@ -414,10 +432,12 @@
             s = 0 if kind == "sum0" else 1
             at = pl.ds(k * rows_h, rows_h)
             src, dst = half_out.at[s, at], half_in.at[s, at]
+        elif kind == "out":
+            at = pl.ds(k * rows_o, rows_o)
+            src, dst = own_out.at[0, at], own_in.at[0, at]
         else:
-            s = 0 if kind == "out" else 1
-            at = pl.ds(k * rows_o, rows_o)
-            src, dst = own_out.at[s, at], own_in.at[s, at]
+            at = at_own_block(k)
+            src, dst = own_out.at[1, at], own_in.at[1, at]
         return copy_to(far, src, dst, link_send.at[n, k], link_recv.at[n, k])
 
     def core(kind, k):
@@ -457,6 +477,7 @@
     loop_rows(width, COL_STEP, pack)
     acc[...] = jnp.zeros_like(acc)
     acc_0[...] = jnp.zeros_like(acc_0)
+    red[...] = jnp.zeros_like(red)
     cent_rows = cent_ref[...].astype(F32)
     cent_at = lax.broadcasted_iota(jnp.int32, cent_rows.shape, 0)
     cent = jnp.sum(jnp.where(cent_at == e, cent_rows, 0.0), axis=0, keepdims=True)
@@ -472,8 +493,7 @@
             route(kind, m).start()
     mine = rows_at(e * capacity, capacity, capacity)
     xa[at_block(0)] = pack_x[mine]
-    first_k, first_i = place[0]
-    ct_own[pl.ds(first_k * rows_o + first_i * capacity, capacity)] = pack_ct[mine]
+    ct_own[at_own_block(0)] = pack_ct[mine]
 
     def send_x(m):
         if m:
@@ -483,8 +503,7 @@
     def send_g(m):
         if m:
             route("ct", m).wait_recv()
-        k, i = place[m]
-        at_o = pl.ds(k * rows_o + i * capacity, capacity)
+        at_o = at_own_block(m)
         values = xa[at_block(m)].astype(F32)
         gate = jax.nn.sigmoid(jnp.sum(values * cent, axis=-1, keepdims=True))
         gate_s[at_o] = jnp.broadcast_to(gate, (capacity, 128))
@@ -506,21 +525,21 @@
         def norm(start, step):
             at = rows_at(k * rows_m + start, step, step)
             rhat, _ = normalize(rows_ref[at].astype(F32))
-            n_s[j, at] = (rhat * gain + bias).astype(BF16)
+            n_s[j][at] = (rhat * gain + bias).astype(BF16)
 
         loop_tiles(rows_m, 2 * ROW_STEP, norm)
 
         def up(start, step):
             cols = rows_at(start, step, step)
-            pre = dot(n_s[j, at_all(k)], up_w[j, :, cols], NN) + up_bias_ref[j : j + 1, cols].astype(
+            pre = dot(n_s[j][at_all(k)], up_w[j, :, cols], NN) + up_bias_ref[j : j + 1, cols].astype(
                 F32
             )
             cdf = 0.5 * (1.0 + lax.erf(pre * (0.5**0.5)))
             pdf = jnp.exp(-0.5 * pre * pre) * 0.3989422804014327
-            a_s[j, at_all(k), cols] = (pre * cdf).astype(BF16)
-            d_s[j, at_all(k), cols] = (cdf + pre * pdf).astype(BF16)
-
-        loop_tiles(hidden, 2 * COL_STEP, up)
+            a_s[j][at_all(k), cols] = (pre * cdf).astype(BF16)
+            d_s[j][at_all(k), cols] = (cdf + pre * pdf).astype(BF16)
+
+        loop_rows(hidden, COL_STEP, up)
 
     def down_step(j, k):
         kind = "part%d" % j
@@ -529,7 +548,7 @@
 
         def down(start, step):
             cols = rows_at(start, step, step)
-            part[0, at_all(k), cols] = dot(a_s[j, at_all(k)], down_w[j, :, cols], NN).astype(BF16)
+            part[0, at_all(k), cols] = dot(a_s[j][at_all(k)], down_w[j, :, cols], NN).astype(BF16)
 
         loop_tiles(width, 2 * COL_STEP, down)
         core(kind, k).start()
@@ -542,13 +561,13 @@
         def act(start, step):
             cols = rows_at(start, step, step)
             grad = dot(grads_ref[at_all(k)], down_w[j, cols, :], NT)
-            d_s[j, at_all(k), cols] = (grad * d_s[j, at_all(k), cols].astype(F32)).astype(BF16)
+            d_s[j][at_all(k), cols] = (grad * d_s[j][at_all(k), cols].astype(F32)).astype(BF16)
 
         loop_tiles(hidden, 2 * COL_STEP, act)
 
         def up_back(start, step):
             cols = rows_at(start, step, step)
-            part[1, at_all(k), cols] = dot(d_s[j, at_all(k)], up_w[j, cols, :], NT).astype(BF16)
+            part[1, at_all(k), cols] = dot(d_s[j][at_all(k)], up_w[j, cols, :], NT).astype(BF16)
 
         loop_tiles(width, 2 * COL_STEP, up_back)
         core(kind, k).start()
@@ -580,7 +599,11 @@
             own_out[o, at_o] = total.astype(BF16)
 
         loop_rows(rows_o, ROW_STEP, add_far)
-        link(link_kind, k).start()
+        if link_kind in BLOCK_KINDS:
+            for m in reversed(order[k]):
+                link(link_kind, m).start()
+        else:
+            link(link_kind, k).start()
 
     def sum_own(s, o, k, start, step):
         at = rows_at(k * rows_m + own + start, step, step)
@@ -626,14 +649,12 @@
         loop_tiles(rows_h, ROW_STEP, grad_h)
         core("hgrad", k).start()
 
-    def give_back(kind, k):
-        for m in order[k]:
-            if m:
-                route(kind, m).start()
-            else:
-                s = 0 if kind == "mixed" else 1
-                _, i = place[0]
-                back_in[s, mine] = back_out[s, pl.ds(k * rows_o + i * capacity, capacity)]
+    def give_back(kind, m):
+        if m:
+            route(kind, m).start()
+        else:
+            s = 0 if kind == "mixed" else 1
+            back_in[s, mine] = back_out[s, at_own_block(0)]
 
     def make_mixed(k):
         link("out", k).wait_recv()
@@ -652,26 +673,32 @@
             acc[2:3] += jnp.sum(lgrad * rows, axis=0, keepdims=True)
 
         loop_rows(rows_o, ROW_STEP, mix)
-        give_back("mixed", k)
-
-    def make_tgrad(k):
-        link("ngrad0", k).wait_recv()
-        gain = gain_ref[0:1].astype(F32)
-
-        def grad_t(start, step):
-            at = rows_at(k * rows_m + own + start, step, step)
-            at_o = rows_at(k * rows_o + start, step, step)
-            ngrad = sum_own(1, 1, k, start, step)
-            back, rhat = norm_back(xa[at].astype(F32), ngrad, gain)
-            back = (hga[at].astype(F32) + back).astype(BF16).astype(F32)
-            back_out[1, at_o] = (
-                ct_own[at_o].astype(F32) + lg_s[at_o][:, 0:1] * cent + back
-            ).astype(BF16)
+        for m in reversed(order[k]):
+            give_back("mixed", m)
+
+    def norm_sums(k):
+        def sum_rows(start, step):
+            at = rows_at(k * rows_m + half + start, step, step)
+            at_h = rows_at(k * rows_h + start, step, step)
+            ngrad = part[1, at].astype(F32) + part_in[1, at_h].astype(F32)
+            rhat, _ = normalize(xa[at].astype(F32))
             acc_0[0:1] += jnp.sum(ngrad * rhat, axis=0, keepdims=True)
             acc_0[1:2] += jnp.sum(ngrad, axis=0, keepdims=True)
 
-        loop_rows(rows_o, ROW_STEP, grad_t)
-        give_back("tgrad", k)
+        loop_tiles(rows_h, ROW_STEP, sum_rows)
+
+    def make_tgrad(m):
+        link("ngrad0", m).wait_recv()
+        k, i = place[m]
+        at_o = at_own_block(m)
+        at = at_block(m)
+        ngrad = sum_own(1, 1, k, i * capacity, capacity)
+        back, _ = norm_back(xa[at].astype(F32), ngrad, gain_ref[0:1].astype(F32))
+        back = (hga[at].astype(F32) + back).astype(BF16).astype(F32)
+        back_out[1, at_o] = (
+            ct_own[at_o].astype(F32) + lg_s[at_o][:, 0:1] * cent + back
+        ).astype(BF16)
+        give_back("tgrad", m)
 
     def column_sums(rows_ref):
         def one(i, total):
@@ -682,33 +709,45 @@
             0, rows_ref.shape[0] // ROW_STEP, one, jnp.zeros((1, rows_ref.shape[1]), F32)
         )
 
-    def weight_grad(j, q):
-        grads_ref = (hga, ga)[j]
-        into, left, right = (
-            (down_grad_ref, a_s.at[j], grads_ref),
-            (up_grad_ref, n_s.at[j], d_s.at[j]),
-        )[q // 2]
+    def weight_grad(q):
+        into, left, right = ((down_grad_ref, a_1, ga), (up_grad_ref, n_1, d_1))[q // 2]
         if q == 0:
-            small_ref[4 + j : 5 + j] = column_sums(right)
+            small_ref[4:5] = column_sums(right)
         if q == 2:
-            ub_ref[j : j + 1] = column_sums(right)
+            small_ref[5:6] = column_sums(right)
         count = left.shape[1] // 2
 
         def tile(start, step):
             at = rows_at(q % 2 * count + start, step, step)
-            into[j, 0, at] = dot(left[:, at], right[...], TN).astype(BF16)
+            into[at] = dot(left[:, at], right[...], TN).astype(BF16)
 
         loop_tiles(count, COL_STEP, tile)
 
+    lanes = width // 128
+    red_rows = (3 * lanes + 8, 2 * lanes)
+
     def over(s):
-        return copy_to(sib, red.at[s, 0], red.at[s, 1], red_send.at[s, 0], red_recv.at[s, 0])
+        at = pl.ds(0, red_rows[s])
+        return copy_to(
+            sib, red.at[s, 0, at], red.at[s, 1, at], red_send.at[s, 0], red_recv.at[s, 0]
+        )
 
     def across(s):
-        return copy_to(far, red.at[s, 0], red.at[s, 2], red_send.at[s, 1], red_recv.at[s, 1])
+        at = pl.ds(0, red_rows[s])
+        return copy_to(
+            far, red.at[s, 0, at], red.at[s, 2, at], red_send.at[s, 1], red_recv.at[s, 1]
+        )
 
     def total(s, step):
+        rows_ref = (acc, acc_0)[s]
         if step == 0:
-            red[s, 0] = (acc, acc_0)[s][...]
+            for r in range(3 - s):
+                for i in range(lanes):
+                    red[s, 0, r * lanes + i : r * lanes + i + 1] = rows_ref[
+                        r : r + 1, i * 128 : (i + 1) * 128
+                    ]
+            if s == 0:
+                red[s, 0, 3 * lanes : 3 * lanes + 2] = rows_ref[3:5, 0:128]
             over(s).start()
         elif step == 1:
             over(s).wait()
@@ -717,17 +756,15 @@
         else:
             across(s).wait()
             sums = red[s, 0] + red[s, 2]
+            for r in range(2):
+                for i in range(lanes):
+                    small_ref[2 * r + 1 - s : 2 * r + 2 - s, i * 128 : (i + 1) * 128] = sums[
+                        r * lanes + i : r * lanes + i + 1
+                    ]
             if s == 0:
-                small_ref[1:2] = sums[0:1]
-                small_ref[3:4] = sums[1:2]
-                for i in range(width // 128):
-                    totals_in[e, i : i + 1] = sums[2:3, i * 128 : (i + 1) * 128]
-                totals_in[e, 8:10] = sums[3:5, 0:128]
+                totals_in[e, 0 : lanes + 2] = sums[2 * lanes : 3 * lanes + 2]
                 for m in others:
                     route("totals", m).start()
-            else:
-                small_ref[0:1] = sums[0:1]
-                small_ref[2:3] = sums[1:2]
 
     def unpack(s):
         kind, out_ref = (("mixed", mixed_ref), ("tgrad", tgrad_ref))[s]
@@ -766,6 +803,7 @@
 
     def back_0(k):
         core("hgrad", k).wait_recv()
+        hg_0[at_all(k)] = hga[at_all(k)]
         back_step(0, hga, k)
 
     tasks = {
@@ -786,9 +824,9 @@
         "MX": make_mixed,
         "B0": back_0,
         "SQ": functools.partial(sum_far, "ngrad0", "ngrad0"),
+        "GS": norm_sums,
         "TG": make_tgrad,
-        "W1": functools.partial(weight_grad, 1),
-        "W0": functools.partial(weight_grad, 0),
+        "W1": weight_grad,
         "R1": functools.partial(total, 0),
         "R0": functools.partial(total, 1),
         "UP": unpack,
@@ -805,10 +843,10 @@
         for kind in ROUTE_KINDS:
             route(kind, m).wait_send()
     for m in range(groups):
-        for kind in LINK_KINDS[:2]:
+        for kind in BLOCK_KINDS:
             link(kind, m).wait_send()
     for k in steps:
-        for kind in LINK_KINDS[2:]:
+        for kind in LINK_KINDS[len(BLOCK_KINDS) :]:
             link(kind, k).wait_send()
         for kind in CORE_KINDS:
             if kind not in ("part0", "ngrad1"):
@@ -821,9 +859,12 @@
     tgrad_ref,
     totals_ref,
     small_ref,
-    ub_ref,
     up_ref,
     down_ref,
+    n_0,
+    a_0,
+    d_0,
+    hg_0,
     mixed_out,
     tgrad_out,
     cent_out,
@@ -835,35 +876,55 @@
     db_out,
     mass_out,
     load_out,
+    cent_s,
+    rows_s,
     up_wide,
     down_wide,
-    row_sem,
-    out_sem,
+    sem,
+    up_sem,
+    down_sem,
 ):
-    layers, tiles, rows = up_wide.shape[:3]
-    leaving = [
-        pltpu.make_async_copy(mixed_ref, mixed_out, row_sem.at[0]),
-        pltpu.make_async_copy(tgrad_ref, tgrad_out, row_sem.at[1]),
-    ]
-    for move in leaving:
+    leaving = []
+
+    def leave(src, dst, semaphore):
+        move = pltpu.make_async_copy(src, dst, semaphore)
         move.start()
-    for j in range(layers):
-        for n, (src, wide, dst) in enumerate(
-            ((down_ref, down_wide, down_out), (up_ref, up_wide, up_out))
-        ):
-            for t in range(tiles):
-                at = pl.ds(t * rows, rows)
-                wide[j, t] = src[j, 0, at].astype(F32)
-                move = pltpu.make_async_copy(wide.at[j, t], dst.at[j, 0, at], out_sem.at[n, j, t])
-                move.start()
-                leaving.append(move)
-    for i in range(cent_out.shape[1] // 128):
-        cent_out[:, i * 128 : (i + 1) * 128] = totals_ref[:, i]
-    for j in range(layers):
-        gain_out[j] = small_ref[j : j + 1]
-        shift_out[j] = small_ref[2 + j : 3 + j]
-        db_out[j] = small_ref[4 + j : 5 + j]
-        ub_out[j] = ub_ref[j : j + 1]
+        leaving.append(move)
+
+    def widen(ref, wide, dst, semaphore, t):
+        at = pl.ds(t * COL_STEP, COL_STEP)
+        wide[1, at] = ref[at].astype(F32)
+        leave(wide.at[1, at], dst.at[1, 0, at], semaphore.at[1, t])
+
+    def multiply(left, right, wide, dst, semaphore, t):
+        at = pl.ds(t * COL_STEP, COL_STEP)
+        wide[0, at] = dot(left[:, at], right[...], TN)
+        leave(wide.at[0, at], dst.at[0, 0, at], semaphore.at[0, t])
+
+    leave(mixed_ref, mixed_out, sem.at[0])
+    leave(tgrad_ref, tgrad_out, sem.at[1])
+    for t in range(down_wide.shape[1] // COL_STEP):
+        widen(down_ref, down_wide, down_out, down_sem, t)
+        multiply(a_0, hg_0, down_wide, down_out, down_sem, t)
+    for t in range(up_wide.shape[1] // COL_STEP):
+        widen(up_ref, up_wide, up_out, up_sem, t)
+        multiply(n_0, d_0, up_wide, up_out, up_sem, t)
+
+    def column_sums(ref):
+        return jnp.sum(ref[...].astype(F32), axis=0, keepdims=True)
+
+    for i in range(cent_s.shape[1] // 128):
+        cent_s[:, i * 128 : (i + 1) * 128] = totals_ref[:, i]
+    leave(cent_s, cent_out, sem.at[2])
+    for j in range(2):
+        rows_s[0, j] = small_ref[j : j + 1]
+        rows_s[1, j] = small_ref[2 + j : 3 + j]
+    rows_s[2, 0] = column_sums(d_0)
+    rows_s[2, 1] = small_ref[5:6]
+    rows_s[3, 0] = column_sums(hg_0)
+    rows_s[3, 1] = small_ref[4:5]
+    for n, dst in enumerate((gain_out, shift_out, ub_out, db_out)):
+        leave(rows_s.at[n], dst, sem.at[3 + n])
     experts = totals_ref.shape[0]
     diagonal = lax.broadcasted_iota(jnp.int32, (experts, 128), 0) == lax.broadcasted_iota(
         jnp.int32, (experts, 128), 1
@@ -889,6 +950,21 @@
     down_bias,
     cotangent,
 ):
+    if not fused_fits(tokens, centroids, up_weight):
+        return per_device(
+            tokens,
+            lengths,
+            expert_ids,
+            slots,
+            centroids,
+            sublayer_norm_gain,
+            sublayer_norm_bias,
+            up_weight,
+            up_bias,
+            down_weight,
+            down_bias,
+            cotangent,
+        )
     tok_rows, width = tokens.shape
     groups = lax.axis_size("expert")
     batches = lax.axis_size("batch")
@@ -909,12 +985,15 @@
             pltpu.VMEM((tok_rows, width), BF16),
             pltpu.VMEM((groups, 16, 128), F32),
             pltpu.VMEM((8, width), F32),
-            pltpu.VMEM((8, hidden), F32),
-            pltpu.VMEM(up_weight.shape, BF16),
-            pltpu.VMEM(down_weight.shape, BF16),
+            pltpu.VMEM(up_weight.shape[2:], BF16),
+            pltpu.VMEM(down_weight.shape[2:], BF16),
+            pltpu.VMEM((total, width), BF16),
+            pltpu.VMEM((total, hidden), BF16),
+            pltpu.VMEM((total, hidden), BF16),
+            pltpu.VMEM((total, width), BF16),
         ],
         in_specs=[vmem] * 9 + [hbm] * 2,
-        out_specs=[vmem] * 7,
+        out_specs=[vmem] * 10,
         scratch_shapes=[
             pltpu.VMEM((2, width, hidden), BF16),
             pltpu.VMEM((2, hidden, width), BF16),
@@ -925,9 +1004,9 @@
             pltpu.VMEM((total, width), BF16),
             pltpu.VMEM((total, width), BF16),
             pltpu.VMEM((total, width), BF16),
-            pltpu.VMEM((2, total, width), BF16),
-            pltpu.VMEM((2, total, hidden), BF16),
-            pltpu.VMEM((2, total, hidden), BF16),
+            pltpu.VMEM((total, width), BF16),
+            pltpu.VMEM((total, hidden), BF16),
+            pltpu.VMEM((total, hidden), BF16),
             pltpu.VMEM((2, total, width), BF16),
             pltpu.VMEM((2, total // 2, width), BF16),
             pltpu.VMEM((2, total // 2, width), BF16),
@@ -941,7 +1020,7 @@
             pltpu.VMEM((2, tok_rows, width), BF16),
             pltpu.VMEM((8, width), F32),
             pltpu.VMEM((8, width), F32),
-            pltpu.VMEM((2, 3, 8, width), F32),
+            pltpu.VMEM((2, 3, 3 * width // 128 + 8, 128), F32),
             pltpu.VMEM((groups, 16, 128), F32),
             pltpu.SemaphoreType.DMA((4,)),
             pltpu.SemaphoreType.DMA((len(ROUTE_KINDS), groups)),
@@ -954,7 +1033,7 @@
             pltpu.SemaphoreType.DMA((2, 2)),
         ],
         compiler_params=pltpu.CompilerParams(
-            collective_id=0, has_side_effects=True, vmem_limit_bytes=52 << 20
+            collective_id=0, has_side_effects=True, vmem_limit_bytes=46 << 20
         ),
         cost_estimate=pl.CostEstimate(
             flops=24 * total * width * hidden, bytes_accessed=40 << 20, transcendentals=0
@@ -973,7 +1052,6 @@
         down_weight,
     )
     layers = up_weight.shape[0]
-    tiles = 4
     row = jax.ShapeDtypeStruct((layers, 1, width), F32)
     return pl.pallas_call(
         functools.partial(widen_kernel, capacity * groups * batches),
@@ -990,13 +1068,16 @@
             jax.ShapeDtypeStruct((experts,), F32),
             jax.ShapeDtypeStruct((experts,), F32),
         ],
-        in_specs=[vmem] * 7,
-        out_specs=[hbm, hbm, vmem, vmem, vmem, hbm, vmem, hbm, vmem, vmem, vmem],
+        in_specs=[vmem] * 10,
+        out_specs=[hbm] * 9 + [vmem] * 2,
         scratch_shapes=[
-            pltpu.VMEM((layers, tiles, width // tiles, hidden), F32),
-            pltpu.VMEM((layers, tiles, hidden // tiles, width), F32),
-            pltpu.SemaphoreType.DMA((2,)),
-            pltpu.SemaphoreType.DMA((2, layers, tiles)),
+            pltpu.VMEM((experts, width), F32),
+            pltpu.VMEM((4, layers, 1, width), F32),
+            pltpu.VMEM((layers, width, hidden), F32),
+            pltpu.VMEM((layers, hidden, width), F32),
+            pltpu.SemaphoreType.DMA((7,)),
+            pltpu.SemaphoreType.DMA((layers, width // COL_STEP)),
+            pltpu.SemaphoreType.DMA((layers, hidden // COL_STEP)),
         ],
         compiler_params=pltpu.CompilerParams(vmem_limit_bytes=24 << 20),
         cost_estimate=pl.CostEstimate(
@@ -1033,7 +1114,6 @@
         P(),
         P(),
     )
-    body = per_device_fused if fused_fits(mesh) else per_device
     return jax.shard_map(
-        body, mesh=mesh, in_specs=in_specs, out_specs=out_specs, check_vma=False
+        per_device_fused, mesh=mesh, in_specs=in_specs, out_specs=out_specs, check_vma=False
     )

time: 120 us -> 116 us (0.967)
  Pallas kernels: 119 us -> 115 us
    pallas_call x1, Pallas kernels: 112 us -> 108 us  [per_device_fused(): pl.pallas_call(functools.partial(fused_kernel, groups, capacity, chunks),...]
where the time goes in v1:
time: 116 us
  Pallas kernels  115 us (99%)
    pallas_call x1, Pallas kernels, per_device_fused(): pl.pallas_call(functools.partial(fused_kernel, groups, capacity, chunks),...  108 us
    pallas_call x1, Pallas kernels, per_device_fused(): pl.pallas_call(functools.partial(widen_kernel, capacity * groups * batche...  7.3 us

profile of v1, /device:TPU:0, one launch (start us, length us, event | category | flops | bytes accessed | tf_op | source)
XLA Modules:
  0.0 116.0 jit_solution(3713636137626170437)
XLA Ops:
  0.6 107.8 %shard_map.194 = (bf16[256,1024]{1,0:T(8,128)(2,1)S(1)}, bf16[256,1024]{1,0:T(8,128)(2,1)S(1)}, f32[8,16,128]{2,1,0:T(8,128)S(1)}, f32[8,1024]{1,0:T(8,128)S(1)}...) custom-call(s32[1,256]{1,0:T(1,128)} %bitcast.10, ...), custom_call_target="tpu_custom_call" | custom-call | flops 25769803776 | bytes 41943040 | tf_op jit(solution)/shard_map/pallas_call | solution.py:981
  108.5 7.3 %shard_map.195 = (bf16[256,1024]{1,0:T(8,128)(2,1)}, bf16[256,1024]{1,0:T(8,128)(2,1)}, f32[8,1024]{1,0:T(8,128)}, f32[2,1,1024]{2,1,0:T(1,128)}, f32[2,1,1024]{...) custom-call(bf16[256,1024]{1,0:T(8,128)(2,1)S(1)} %get-tuple-element, ...), custom_call_target="tpu_custom_call" | custom-call | bytes 25165824 | tf_op jit(solution)/shard_map/pallas_call | solution.py:1056

commit v2 on v1

--- a/solution.py
+++ b/solution.py
@@ -208,31 +208,35 @@
 LINK_KINDS = BLOCK_KINDS + ("sum0", "out", "ngrad1")
 CORE_KINDS = ("x", "g", "part0", "h", "part1", "ngrad1", "hgrad", "ngrad0")
 SCHEDULE = (
-    "SX.0 SG.0 SX.1 SX.2",
-    "SX.3 SX.4 SX.5 SG.2",
-    "SG.1 PX.0 U0.0 SX.6",
-    "SG.3 D0.0 PX.1 S0.0",
-    "U0.1 D0.1 PX.3 SX.7",
-    "SG.5 S0.1 PX.2 H.0",
-    "PG.3 U0.3 PG.0 SG.4",
-    "U0.2 D0.2 SG.7 D0.3",
-    "SG.6 PG.1 S0.2 U1.0",
-    "PG.2 H.1 S0.3 U1.1",
-    "B1.0 D1.1 H.2 S1.0",
-    "B1.1 U1.2 S1.1 H.3",
-    "SO.1 B1.2 U1.3 B1.3",
-    "W1.2 S1.2 D1.0 HG.1",
-    "HG.0 W1.0 SO.0 B0.1",
-    "B0.0 MX.1 SQ.1 GS.1",
-    "S1.3 HG.2 W1.3 B0.2",
-    "D1.2 D1.3 SO.2 TG.5",
-    "TG.4 MX.0 SQ.2 GS.2",
-    "HG.3 SO.3 SQ.0 GS.0",
-    "W1.1 MX.2 B0.3 TG.7",
-    "TG.6 SQ.3 GS.3 R0.0",
-    "MX.3 R1.0 R1.1 TG.3",
-    "TG.2 TG.1 TG.0 R1.2",
-    "UP.0 R0.1 R0.2 UP.1",
+    "RX.1 RX.2 RX.3 RC.1",
+    "RX.4 RX.5 RX.6 RX.7",
+    "RC.2 RC.3 RC.4 RC.5",
+    "RC.6 RC.7 SX.0 SG.0",
+    "SX.1 SX.2 SX.3 SX.4",
+    "SX.5 PX.3 PX.0 SG.2",
+    "SX.6 SG.1 U0.0 PX.1",
+    "D0.0 SX.7 SG.3 U0.1",
+    "S0.0 U0.3 D0.1 PX.2",
+    "S0.1 U0.2 SG.5 SG.4",
+    "H.0 D0.2 D0.3 SG.7",
+    "S0.3 H.1 S0.2 U1.1",
+    "SG.6 PG.0 D1.1 U1.0",
+    "SO.1 PG.1 H.3 B1.1",
+    "D1.0 B1.0 H.2 S1.1",
+    "U1.2 S1.0 PG.3 PG.2",
+    "U1.3 D1.2 B1.2 HG.1",
+    "S1.2 B1.3 MX.1 B0.1",
+    "W1.3 SO.2 HG.0 SQ.1",
+    "B0.0 S1.3 HG.2 D1.3",
+    "SO.0 GS.1 TG.5 B0.2",
+    "SO.3 TG.4 W1.0 MX.2",
+    "SQ.2 GS.2 HG.3 W1.2",
+    "SQ.0 B0.3 MX.0 MX.3",
+    "R1.0 TG.7 GS.0 TG.6",
+    "R1.1 SQ.3 GS.3 R0.0",
+    "TG.3 R0.1 R1.2 TG.2",
+    "TG.1 R0.2 TG.0 W1.1",
+    "UP.0 UP.1",
 )
 PART_SLOT = {"part0": 0, "part1": 0, "ngrad1": 1, "ngrad0": 1}
 ROUTE_KINDS = ("x", "ct", "mixed", "tgrad", "totals")
@@ -289,15 +293,15 @@
     groups,
     capacity,
     chunks,
-    ids_ref,
-    slots_ref,
-    tok_ref,
-    ct_ref,
-    cent_ref,
-    gain_ref,
-    bias_ref,
-    up_bias_ref,
-    down_bias_ref,
+    ids_hbm,
+    slots_hbm,
+    tok_hbm,
+    ct_hbm,
+    cent_hbm,
+    gain_hbm,
+    bias_hbm,
+    up_bias_hbm,
+    down_bias_hbm,
     up_hbm,
     down_hbm,
     mixed_ref,
@@ -310,6 +314,15 @@
     a_0,
     d_0,
     hg_0,
+    ids_ref,
+    slots_ref,
+    tok_ref,
+    ct_ref,
+    cent_ref,
+    gain_ref,
+    bias_ref,
+    up_bias_ref,
+    down_bias_ref,
     up_w,
     down_w,
     perm,
@@ -337,6 +350,7 @@
     acc_0,
     red,
     totals_in,
+    in_sem,
     w_sem,
     route_send,
     route_recv,
@@ -455,12 +469,33 @@
     peers = [sib, far] + [(flipped(m), b) for m in range(1, groups)]
     for peer in peers:
         pl.semaphore_signal(barrier, inc=1, device_id=peer, device_id_type=MESH)
+    arrivals = [
+        pltpu.make_async_copy(src, dst, in_sem.at[n])
+        for n, (src, dst) in enumerate(
+            (
+                (ids_hbm, ids_ref),
+                (slots_hbm, slots_ref),
+                (tok_hbm, tok_ref),
+                (ct_hbm, ct_ref),
+                (cent_hbm, cent_ref),
+                (gain_hbm, gain_ref),
+                (bias_hbm, bias_ref),
+                (up_bias_hbm, up_bias_ref),
+                (down_bias_hbm, down_bias_ref),
+            )
+        )
+    ]
     loads = []
     for j in range(2):
         loads.append(pltpu.make_async_copy(up_hbm.at[j, 0], up_w.at[j], w_sem.at[2 * j]))
         loads.append(pltpu.make_async_copy(down_hbm.at[j, 0], down_w.at[j], w_sem.at[2 * j + 1]))
-    for load in loads:
+    for load in arrivals + loads:
         load.start()
+    acc[...] = jnp.zeros_like(acc)
+    acc_0[...] = jnp.zeros_like(acc_0)
+    red[...] = jnp.zeros_like(red)
+    arrivals[0].wait()
+    arrivals[1].wait()
     target = jnp.where(
         slots_ref[...] >= 0, ids_ref[...] * capacity + slots_ref[...], -1
     )
@@ -469,28 +504,24 @@
     perm[...] = onehot.astype(BF16)
     empty = EMPTY * (1.0 - jnp.sum(onehot, axis=1, keepdims=True))
 
-    def pack(start, step):
+    def pack_tokens(start, step):
         cols = rows_at(start, step, step)
         pack_x[:, cols] = (dot(perm[...], tok_ref[:, cols], NN) + empty).astype(BF16)
+
+    def pack_cotangent(start, step):
+        cols = rows_at(start, step, step)
         pack_ct[:, cols] = dot(perm[...], ct_ref[:, cols], NN).astype(BF16)
 
-    loop_rows(width, COL_STEP, pack)
-    acc[...] = jnp.zeros_like(acc)
-    acc_0[...] = jnp.zeros_like(acc_0)
-    red[...] = jnp.zeros_like(red)
+    arrivals[2].wait()
+    loop_rows(width, COL_STEP, pack_tokens)
+    arrivals[3].wait()
+    loop_rows(width, COL_STEP, pack_cotangent)
+    for arrival in arrivals[4:]:
+        arrival.wait()
     cent_rows = cent_ref[...].astype(F32)
     cent_at = lax.broadcasted_iota(jnp.int32, cent_rows.shape, 0)
     cent = jnp.sum(jnp.where(cent_at == e, cent_rows, 0.0), axis=0, keepdims=True)
     pl.semaphore_wait(barrier, len(peers))
-    near = 2 * per
-    for kind, masks in (
-        ("x", range(1, near)),
-        ("ct", range(1, per)),
-        ("x", range(near, groups)),
-        ("ct", range(per, groups)),
-    ):
-        for m in masks:
-            route(kind, m).start()
     mine = rows_at(e * capacity, capacity, capacity)
     xa[at_block(0)] = pack_x[mine]
     ct_own[at_own_block(0)] = pack_ct[mine]
@@ -807,6 +838,8 @@
         back_step(0, hga, k)
 
     tasks = {
+        "RX": lambda m: route("x", m).start(),
+        "RC": lambda m: route("ct", m).start(),
         "SX": send_x,
         "SG": send_g,
         "PX": functools.partial(spread, "x"),
@@ -992,9 +1025,18 @@
             pltpu.VMEM((total, hidden), BF16),
             pltpu.VMEM((total, width), BF16),
         ],
-        in_specs=[vmem] * 9 + [hbm] * 2,
+        in_specs=[pl.BlockSpec(memory_space=pltpu.HBM)] * 11,
         out_specs=[vmem] * 10,
         scratch_shapes=[
+            pltpu.VMEM((1, tok_rows), jnp.int32),
+            pltpu.VMEM((1, tok_rows), jnp.int32),
+            pltpu.VMEM((tok_rows, width), BF16),
+            pltpu.VMEM((tok_rows, width), BF16),
+            pltpu.VMEM((experts, width), BF16),
+            pltpu.VMEM((2, width), BF16),
+            pltpu.VMEM((2, width), BF16),
+            pltpu.VMEM((2, hidden), BF16),
+            pltpu.VMEM((2, width), BF16),
             pltpu.VMEM((2, width, hidden), BF16),
             pltpu.VMEM((2, hidden, width), BF16),
             pltpu.VMEM((tok_rows, tok_rows), BF16),
@@ -1022,6 +1064,7 @@
             pltpu.VMEM((8, width), F32),
             pltpu.VMEM((2, 3, 3 * width // 128 + 8, 128), F32),
             pltpu.VMEM((groups, 16, 128), F32),
+            pltpu.SemaphoreType.DMA((9,)),
             pltpu.SemaphoreType.DMA((4,)),
             pltpu.SemaphoreType.DMA((len(ROUTE_KINDS), groups)),
             pltpu.SemaphoreType.DMA((len(ROUTE_KINDS), groups)),

time: 116 us -> 115 us (level)
    pallas_call x1, Pallas kernels: 108 us -> 106 us  [per_device_fused(): pl.pallas_call(functools.partial(fused_kernel, groups, capacity, chunks),...]
where the time goes in v2:
time: 115 us; the launch traced here: 114 us
  Pallas kernels  114 us (99%)
    pallas_call x1, Pallas kernels, per_device_fused(): pl.pallas_call(functools.partial(fused_kernel, groups, capacity, chunks),...  106 us
    pallas_call x1, Pallas kernels, per_device_fused(): pl.pallas_call(functools.partial(widen_kernel, capacity * groups * batche...  7.3 us

profile of v2, /device:TPU:0, one launch (start us, length us, event | category | flops | bytes accessed | tf_op | source)
XLA Modules:
  0.0 114.3 jit_solution(1468246354322386291)
XLA Ops:
  0.6 106.2 %shard_map.194 = (bf16[256,1024]{1,0:T(8,128)(2,1)S(1)}, bf16[256,1024]{1,0:T(8,128)(2,1)S(1)}, f32[8,16,128]{2,1,0:T(8,128)S(1)}, f32[8,1024]{1,0:T(8,128)S(1)}...) custom-call(s32[1,256]{1,0:T(1,128)} %bitcast.10, ...), custom_call_target="tpu_custom_call" | custom-call | flops 25769803776 | bytes 41943040 | tf_op jit(solution)/shard_map/pallas_call | solution.py:1014
  106.9 7.3 %shard_map.195 = (bf16[256,1024]{1,0:T(8,128)(2,1)}, bf16[256,1024]{1,0:T(8,128)(2,1)}, f32[8,1024]{1,0:T(8,128)}, f32[2,1,1024]{2,1,0:T(1,128)}, f32[2,1,1024]{...) custom-call(bf16[256,1024]{1,0:T(8,128)(2,1)S(1)} %get-tuple-element, ...), custom_call_target="tpu_custom_call" | custom-call | bytes 25165824 | tf_op jit(solution)/shard_map/pallas_call | solution.py:1099

commit v3 on v2

--- a/solution.py
+++ b/solution.py
@@ -208,35 +208,35 @@
 LINK_KINDS = BLOCK_KINDS + ("sum0", "out", "ngrad1")
 CORE_KINDS = ("x", "g", "part0", "h", "part1", "ngrad1", "hgrad", "ngrad0")
 SCHEDULE = (
-    "RX.1 RX.2 RX.3 RC.1",
-    "RX.4 RX.5 RX.6 RX.7",
-    "RC.2 RC.3 RC.4 RC.5",
-    "RC.6 RC.7 SX.0 SG.0",
-    "SX.1 SX.2 SX.3 SX.4",
-    "SX.5 PX.3 PX.0 SG.2",
-    "SX.6 SG.1 U0.0 PX.1",
-    "D0.0 SX.7 SG.3 U0.1",
-    "S0.0 U0.3 D0.1 PX.2",
-    "S0.1 U0.2 SG.5 SG.4",
-    "H.0 D0.2 D0.3 SG.7",
-    "S0.3 H.1 S0.2 U1.1",
-    "SG.6 PG.0 D1.1 U1.0",
-    "SO.1 PG.1 H.3 B1.1",
-    "D1.0 B1.0 H.2 S1.1",
-    "U1.2 S1.0 PG.3 PG.2",
-    "U1.3 D1.2 B1.2 HG.1",
-    "S1.2 B1.3 MX.1 B0.1",
-    "W1.3 SO.2 HG.0 SQ.1",
-    "B0.0 S1.3 HG.2 D1.3",
-    "SO.0 GS.1 TG.5 B0.2",
-    "SO.3 TG.4 W1.0 MX.2",
-    "SQ.2 GS.2 HG.3 W1.2",
-    "SQ.0 B0.3 MX.0 MX.3",
-    "R1.0 TG.7 GS.0 TG.6",
-    "R1.1 SQ.3 GS.3 R0.0",
-    "TG.3 R0.1 R1.2 TG.2",
-    "TG.1 R0.2 TG.0 W1.1",
-    "UP.0 UP.1",
+    "RX.1 RX.2 RX.3 RX.4",
+    "RX.5 RX.6 RX.7 SX.0",
+    "PC.0 RC.1 RC.2 RC.3",
+    "RC.4 RC.5 RC.6 RC.7",
+    "SG.0 SX.1 SX.2 SX.3",
+    "SX.4 SX.5 PX.3 PX.0",
+    "SG.2 SX.6 SG.1 U0.0",
+    "PX.1 D0.0 SX.7 SG.3",
+    "U0.1 S0.0 U0.3 D0.1",
+    "PX.2 S0.1 U0.2 SG.5",
+    "SG.4 H.0 D0.2 D0.3",
+    "SG.7 S0.3 H.1 S0.2",
+    "U1.1 SG.6 PG.0 D1.1",
+    "U1.0 SO.1 PG.1 H.3",
+    "B1.1 D1.0 B1.0 H.2",
+    "S1.1 U1.2 S1.0 PG.3",
+    "PG.2 U1.3 D1.2 B1.2",
+    "HG.1 S1.2 B1.3 MX.1",
+    "B0.1 W1.3 SO.2 HG.0",
+    "SQ.1 B0.0 S1.3 HG.2",
+    "D1.3 SO.0 GS.1 TG.5",
+    "B0.2 SO.3 TG.4 W1.0",
+    "MX.2 SQ.2 GS.2 HG.3",
+    "W1.2 SQ.0 B0.3 MX.0",
+    "MX.3 R1.0 TG.7 GS.0",
+    "TG.6 R1.1 SQ.3 GS.3",
+    "R0.0 TG.3 R0.1 R1.2",
+    "TG.2 TG.1 R0.2 TG.0",
+    "W1.1 UP.0 UP.1",
 )
 PART_SLOT = {"part0": 0, "part1": 0, "ngrad1": 1, "ngrad0": 1}
 ROUTE_KINDS = ("x", "ct", "mixed", "tgrad", "totals")
@@ -348,6 +348,7 @@
     back_in,
     acc,
     acc_0,
+    cent_s,
     red,
     totals_in,
     in_sem,
@@ -514,17 +515,19 @@
 
     arrivals[2].wait()
     loop_rows(width, COL_STEP, pack_tokens)
-    arrivals[3].wait()
-    loop_rows(width, COL_STEP, pack_cotangent)
-    for arrival in arrivals[4:]:
-        arrival.wait()
-    cent_rows = cent_ref[...].astype(F32)
-    cent_at = lax.broadcasted_iota(jnp.int32, cent_rows.shape, 0)
-    cent = jnp.sum(jnp.where(cent_at == e, cent_rows, 0.0), axis=0, keepdims=True)
     pl.semaphore_wait(barrier, len(peers))
     mine = rows_at(e * capacity, capacity, capacity)
     xa[at_block(0)] = pack_x[mine]
-    ct_own[at_own_block(0)] = pack_ct[mine]
+
+    def prepare_cotangent(_):
+        arrivals[3].wait()
+        loop_rows(width, COL_STEP, pack_cotangent)
+        ct_own[at_own_block(0)] = pack_ct[mine]
+        for arrival in arrivals[4:]:
+            arrival.wait()
+        cent_rows = cent_ref[...].astype(F32)
+        cent_at = lax.broadcasted_iota(jnp.int32, cent_rows.shape, 0)
+        cent_s[0:1] = jnp.sum(jnp.where(cent_at == e, cent_rows, 0.0), axis=0, keepdims=True)
 
     def send_x(m):
         if m:
@@ -536,7 +539,7 @@
             route("ct", m).wait_recv()
         at_o = at_own_block(m)
         values = xa[at_block(m)].astype(F32)
-        gate = jax.nn.sigmoid(jnp.sum(values * cent, axis=-1, keepdims=True))
+        gate = jax.nn.sigmoid(jnp.sum(values * cent_s[0:1], axis=-1, keepdims=True))
         gate_s[at_o] = jnp.broadcast_to(gate, (capacity, 128))
         ga[at_block(m)] = (gate * ct_own[at_o].astype(F32)).astype(BF16)
         used = jnp.where(values[:, 0:1] < 7.0, 1.0, 0.0)
@@ -727,7 +730,7 @@
         back, _ = norm_back(xa[at].astype(F32), ngrad, gain_ref[0:1].astype(F32))
         back = (hga[at].astype(F32) + back).astype(BF16).astype(F32)
         back_out[1, at_o] = (
-            ct_own[at_o].astype(F32) + lg_s[at_o][:, 0:1] * cent + back
+            ct_own[at_o].astype(F32) + lg_s[at_o][:, 0:1] * cent_s[0:1] + back
         ).astype(BF16)
         give_back("tgrad", m)
 
@@ -839,6 +842,7 @@
 
     tasks = {
         "RX": lambda m: route("x", m).start(),
+        "PC": prepare_cotangent,
         "RC": lambda m: route("ct", m).start(),
         "SX": send_x,
         "SG": send_g,
@@ -911,6 +915,7 @@
     load_out,
     cent_s,
     rows_s,
+    vec_s,
     up_wide,
     down_wide,
     sem,
@@ -962,9 +967,10 @@
     diagonal = lax.broadcasted_iota(jnp.int32, (experts, 128), 0) == lax.broadcasted_iota(
         jnp.int32, (experts, 128), 1
     )
-    for out, n in ((mass_out, 8), (load_out, 9)):
+    for i, (dst, n) in enumerate(((mass_out, 8), (load_out, 9))):
         values = jnp.sum(jnp.where(diagonal, totals_ref[:, n], 0.0), axis=0)
-        out[...] = values[0:experts] / jnp.float32(denominator)
+        vec_s[i, 0:experts] = values[0:experts] / jnp.float32(denominator)
+        leave(vec_s.at[i], dst, sem.at[7 + i])
     for move in leaving:
         move.wait()
 
@@ -1062,6 +1068,7 @@
             pltpu.VMEM((2, tok_rows, width), BF16),
             pltpu.VMEM((8, width), F32),
             pltpu.VMEM((8, width), F32),
+            pltpu.VMEM((8, width), F32),
             pltpu.VMEM((2, 3, 3 * width // 128 + 8, 128), F32),
             pltpu.VMEM((groups, 16, 128), F32),
             pltpu.SemaphoreType.DMA((9,)),
@@ -1112,13 +1119,14 @@
             jax.ShapeDtypeStruct((experts,), F32),
         ],
         in_specs=[vmem] * 10,
-        out_specs=[hbm] * 9 + [vmem] * 2,
+        out_specs=[hbm] * 11,
         scratch_shapes=[
             pltpu.VMEM((experts, width), F32),
             pltpu.VMEM((4, layers, 1, width), F32),
+            pltpu.VMEM((2, experts), F32),
             pltpu.VMEM((layers, width, hidden), F32),
             pltpu.VMEM((layers, hidden, width), F32),
-            pltpu.SemaphoreType.DMA((7,)),
+            pltpu.SemaphoreType.DMA((9,)),
             pltpu.SemaphoreType.DMA((layers, width // COL_STEP)),
             pltpu.SemaphoreType.DMA((layers, hidden // COL_STEP)),
         ],

time: 115 us -> 114 us (level)
  no operation moved by 1% of the time
where the time goes in v3:
time: 114 us
  Pallas kernels  113 us (99%)
    pallas_call x1, Pallas kernels, per_device_fused(): pl.pallas_call(functools.partial(fused_kernel, groups, capacity, chunks),...  106 us
    pallas_call x1, Pallas kernels, per_device_fused(): pl.pallas_call(functools.partial(widen_kernel, capacity * groups * batche...  6.81 us

profile of v3, /device:TPU:0, one launch (start us, length us, event | category | flops | bytes accessed | tf_op | source)
XLA Modules:
  0.0 113.5 jit_solution(14121406945574008038)
XLA Ops:
  0.6 105.9 %shard_map.194 = (bf16[256,1024]{1,0:T(8,128)(2,1)S(1)}, bf16[256,1024]{1,0:T(8,128)(2,1)S(1)}, f32[8,16,128]{2,1,0:T(8,128)S(1)}, f32[8,1024]{1,0:T(8,128)S(1)}...) custom-call(s32[1,256]{1,0:T(1,128)} %bitcast.10, ...), custom_call_target="tpu_custom_call" | custom-call | flops 25769803776 | bytes 41943040 | tf_op jit(solution)/shard_map/pallas_call | solution.py:1020
  106.5 6.8 %shard_map.195 = (bf16[256,1024]{1,0:T(8,128)(2,1)}, bf16[256,1024]{1,0:T(8,128)(2,1)}, f32[8,1024]{1,0:T(8,128)}, f32[2,1,1024]{2,1,0:T(1,128)}, f32[2,1,1024]{...) custom-call(bf16[256,1024]{1,0:T(8,128)(2,1)S(1)} %get-tuple-element, ...), custom_call_target="tpu_custom_call" | custom-call | bytes 25165824 | tf_op jit(solution)/shard_map/pallas_call | solution.py:1106

commit v4 on v3

--- a/solution.py
+++ b/solution.py
@@ -235,8 +235,8 @@
     "MX.3 R1.0 TG.7 GS.0",
     "TG.6 R1.1 SQ.3 GS.3",
     "R0.0 TG.3 R0.1 R1.2",
-    "TG.2 TG.1 R0.2 TG.0",
-    "W1.1 UP.0 UP.1",
+    "TG.2 TG.1 W1.1 TG.0",
+    "UP.0 R0.2 UP.1",
 )
 PART_SLOT = {"part0": 0, "part1": 0, "ngrad1": 1, "ngrad0": 1}
 ROUTE_KINDS = ("x", "ct", "mixed", "tgrad", "totals")

time: 114 us -> 114 us (level)
  no operation moved by 1% of the time
where the time goes in v4:
time: 114 us
  Pallas kernels  113 us (99%)
    pallas_call x1, Pallas kernels, per_device_fused(): pl.pallas_call(functools.partial(fused_kernel, groups, capacity, chunks),...  106 us
    pallas_call x1, Pallas kernels, per_device_fused(): pl.pallas_call(functools.partial(widen_kernel, capacity * groups * batche...  6.81 us

profile of v4, /device:TPU:0, one launch (start us, length us, event | category | flops | bytes accessed | tf_op | source)
XLA Modules:
  0.0 113.5 jit_solution(163471844288173324)
XLA Ops:
  0.6 105.9 %shard_map.194 = (bf16[256,1024]{1,0:T(8,128)(2,1)S(1)}, bf16[256,1024]{1,0:T(8,128)(2,1)S(1)}, f32[8,16,128]{2,1,0:T(8,128)S(1)}, f32[8,1024]{1,0:T(8,128)S(1)}...) custom-call(s32[1,256]{1,0:T(1,128)} %bitcast.10, ...), custom_call_target="tpu_custom_call" | custom-call | flops 25769803776 | bytes 41943040 | tf_op jit(solution)/shard_map/pallas_call | solution.py:1020
  106.5 6.8 %shard_map.195 = (bf16[256,1024]{1,0:T(8,128)(2,1)}, bf16[256,1024]{1,0:T(8,128)(2,1)}, f32[8,1024]{1,0:T(8,128)}, f32[2,1,1024]{2,1,0:T(1,128)}, f32[2,1,1024]{...) custom-call(bf16[256,1024]{1,0:T(8,128)(2,1)S(1)} %get-tuple-element, ...), custom_call_target="tpu_custom_call" | custom-call | bytes 25165824 | tf_op jit(solution)/shard_map/pallas_call | solution.py:1106
